TPU v7x, 32 devices: a whole 2x2x4 slice. The times are simulated.
32 devices in a mesh: tm: 4 (over y, x), row: 4 (over z), col: 2 (over core).
Axes of the slice: x: 2, y: 2, z: 4, core: 2. Of those that a mesh axis runs over, the one named last changes fastest.
Arguments:
- features: float32 [8, 32, 64, 128], P('tm', 'row', 'col'), may hold values from -100 to 100
- gain_first: float32 [128], replicated, may hold values from 0.1 to 1.9
- shift_first: float32 [128], replicated, may hold values from -3 to 3
- weight_first: float32 [3, 3, 3, 128, 128], replicated, may hold values from -0.109375 to 0.109375
- gain_second: float32 [128], replicated, may hold values from 0.1 to 1.9
- shift_second: float32 [128], replicated, may hold values from -3 to 3
- weight_second: float32 [3, 3, 3, 128, 128], replicated, may hold values from -0.109375 to 0.109375
- bias_second: float32 [128], replicated, may hold values from -3 to 3
Outputs:
- encoded: float32 [8, 32, 64, 128], P('tm', 'row', 'col')
All inputs are finite; a program needn't handle non-finite values.
Results may differ from a plain program's by a relative error of at most 0.00005.
Values sent between devices are 32-bit elements; how exact they have to be, the bound alone decides.
A program may use at most 64 MiB of HBM per device.

v0:
```python
import jax
import jax.numpy as jnp
from jax import lax
from jax.sharding import PartitionSpec as P

GROUPS = 32


epsilon = 1e-06


def shifted(value, axis, steps):
    count = lax.axis_size(axis)
    first, last = (max(0, -steps), min(count, count - steps))
    return lax.ppermute(value, axis, [(source, source + steps) for source in range(first, last)])


def padded_2(array, sides, width):
    for axis, dim in sides:
        size, length = (lax.axis_size(axis), array.shape[dim])
        up = [(i, (i + 1) % size) for i in range(size - 1)]
        down = [(j, i) for i, j in up]
        last = lax.slice_in_dim(array, length - width, length, axis=dim)
        first = lax.slice_in_dim(array, 0, width, axis=dim)
        before = lax.ppermute(last, axis, up)
        after = lax.ppermute(first, axis, down)
        array = jnp.concatenate([before, array, after], axis=dim)
    return array


def group_stats(values):
    channels = values.shape[-1]
    per_group = channels // GROUPS
    flattened = values.reshape(-1, GROUPS, per_group)
    total_count = (
        flattened.shape[0]
        * per_group
        * lax.axis_size("tm")
        * lax.axis_size("row")
        * lax.axis_size("col")
    )
    average = lax.psum(jnp.sum(flattened, axis=(0, 2)), ("tm", "row", "col")) / total_count
    centered = flattened - average[None, :, None]
    spread = lax.psum(jnp.sum(centered * centered, axis=(0, 2)), ("tm", "row", "col")) / total_count
    chan_mean = jnp.repeat(average, per_group)
    chan_scale = jnp.repeat(lax.rsqrt(spread + epsilon), per_group)
    return (chan_mean, chan_scale)


def apply_norm(values, stats, gain, offset):
    chan_mean, chan_scale = stats
    return jax.nn.silu((values - chan_mean) * chan_scale * gain + offset)


def causal_front(block):
    earlier = shifted(block, "tm", 1)
    repeated = jnp.concatenate([block[:1], block[:1]], axis=0)
    front = jnp.where(lax.axis_index("tm") == 0, repeated, earlier)
    return jnp.concatenate([front, block], axis=0)


def conv_valid(padded, weights):
    frames = padded.shape[0] - 2
    height = padded.shape[1] - 2
    width = padded.shape[2] - 2
    channels = padded.shape[3]
    total = jnp.zeros((frames * height * width, weights.shape[-1]), jnp.float32)
    for time_tap in range(3):
        for row_tap in range(3):
            slab = jnp.concatenate(
                [
                    padded[
                        time_tap : time_tap + frames,
                        row_tap : row_tap + height,
                        col_tap : col_tap + width,
                    ]
                    for col_tap in range(3)
                ],
                axis=-1,
            )
            total = total + jnp.dot(
                slab.reshape(-1, 3 * channels),
                weights[time_tap, row_tap].reshape(3 * channels, -1),
                precision=lax.Precision.HIGHEST,
            )
    return total.reshape(frames, height, width, -1)


def local(
    features,
    gain_first,
    shift_first,
    weight_first,
    gain_second,
    shift_second,
    weight_second,
    bias_second,
):
    first_stats = group_stats(features)

    def layer_input(activated):
        widened = padded_2(activated, (("row", 1), ("col", 2)), 1)
        return causal_front(widened)

    first = apply_norm(features, first_stats, gain_first, shift_first)
    hidden = conv_valid(layer_input(first), weight_first)
    second = apply_norm(hidden, group_stats(hidden), gain_second, shift_second)
    branch_out = conv_valid(layer_input(second), weight_second)
    return features + branch_out + bias_second


def solution(mesh):
    in_specs = (P("tm", "row", "col", None), P(), P(), P(), P(), P(), P(), P())
    out_specs = P("tm", "row", "col", None)
    return jax.shard_map(local, mesh=mesh, in_specs=in_specs, out_specs=out_specs, check_vma=False)
```

profile of v0, /device:TPU:0, one launch (start us, length us, event | category | flops | bytes accessed | tf_op | source)
XLA Modules:
  0.0 238.9 jit_solution(3668913208940452636)
XLA Ops:
  0.0 1.0 reduce_sum.46
  1.3 42.0 %psum.28 = f32[32]{0:T(128)S(1)} all-reduce(f32[32]{0:T(128)S(1)} %reduce_sum.51), channel_id=1, replica_groups=mesh['tm'=4,'row'=4,'col'=2] {'tm','row','col'}, use_global_device_ids=true, to_apply=%region_2.0 | all-reduce | flops 32 | bytes 256 | tf_op jit(solution)/shard_map/psum | solution.py:42
  43.5 1.0 multiply_reduce_fusion.1
  44.7 40.2 %psum.29 = f32[32]{0:T(128)S(1)} all-reduce(f32[32]{0:T(128)S(1)} %reduce_sum.54), channel_id=1, replica_groups=mesh['tm'=4,'row'=4,'col'=2] {'tm','row','col'}, use_global_device_ids=true, to_apply=%region_5.6 | all-reduce | flops 32 | bytes 256 | tf_op jit(solution)/shard_map/psum | solution.py:44
  85.1 1.1 divide_multiply_fusion.1
  86.1 1.3 collective-permute-start.1
  87.4 4.5 %collective-permute-start = (f32[2,1,32,128]{3,2,1,0:T(8,128)S(1)}, f32[2,1,32,128]{3,2,1,0:T(8,128)S(1)}, u32[]{:S(2)}, u32[]{:S(2)}) collective-permute-start(f32[2,1,32,128]{3,2,1,0:T(8,128)S(1)} %get-tuple-element.87), channel_id=1, source_target_pairs={{0,2},{2,4},{4,6},{1,3},{3,5},{5,7},{8,10},{10,12},{12,14},{9,11},... | collective-permute-start | bytes 98312 | tf_op jit(solution)/shard_map/ppermute | solution.py:25
  92.0 1.6 collective-permute-done
  93.6 1.3 collective-permute-start.3
  94.9 3.0 %collective-permute-start.2 = (f32[2,10,1,128]{3,2,1,0:T(1,128)S(1)}, f32[2,10,1,128]{3,2,1,0:T(1,128)S(1)}, u32[]{:S(2)}, u32[]{:S(2)}) collective-permute-start(f32[2,10,1,128]{3,2,1,0:T(1,128)S(1)} %get-tuple-element.77), channel_id=1, source_target_pairs={{0,1},{2,3},{4,5},{6,7},{8,9},{10,11},{12,13},{14,15},{16,17},{18,... | collective-permute-start | bytes 30728 | tf_op jit(solution)/shard_map/ppermute | solution.py:25
  97.9 1.6 fusion.9
  99.7 4.2 %collective-permute-start.4 = (f32[2,10,34,128]{3,2,1,0:T(8,128)S(1)}, f32[2,10,34,128]{3,2,1,0:T(8,128)S(1)}, u32[]{:S(2)}, u32[]{:S(2)}) collective-permute-start(f32[2,10,34,128]{3,2,1,0:T(8,128)S(1)} %pad_maximum_fusion.18), channel_id=1, source_target_pairs={{0,8},{8,16},{16,24},{1,9},{9,17},{17,25},{2,10},{10,18},{18,26},{... | collective-permute-start | bytes 1044488 | tf_op jit(solution)/shard_map/ppermute | solution.py:15
  104.4 7.8 %collective-permute-done.4 = f32[2,10,34,128]{3,2,1,0:T(8,128)S(1)} collective-permute-done((f32[2,10,34,128]{3,2,1,0:T(8,128)S(1)}, f32[2,10,34,128]{3,2,1,0:T(8,128)S(1)}, u32[]{:S(2)}, u32[]{:S(2)}) %collective-permute-start.4) | collective-permute-done | bytes 348192 | tf_op jit(solution)/shard_map/ppermute | solution.py:15
  113.8 0.8 convolution_add_fusion.15
  114.7 0.8 convolution_add_fusion.14
  119.0 0.8 convolution_add_fusion.9
  120.9 42.1 %psum.30 = f32[32]{0:T(128)S(1)} all-reduce(f32[32]{0:T(128)S(1)} %reduce_sum.72), channel_id=1, replica_groups=mesh['tm'=4,'row'=4,'col'=2] {'tm','row','col'}, use_global_device_ids=true, to_apply=%region_8.9 | all-reduce | flops 32 | bytes 256 | tf_op jit(solution)/shard_map/psum | solution.py:42
  163.5 39.8 %psum.31 = f32[32]{0:T(128)S(1)} all-reduce(f32[32]{0:T(128)S(1)} %reduce_sum.75), channel_id=1, replica_groups=mesh['tm'=4,'row'=4,'col'=2] {'tm','row','col'}, use_global_device_ids=true, to_apply=%region_11.12 | all-reduce | flops 32 | bytes 256 | tf_op jit(solution)/shard_map/psum | solution.py:44
  203.6 1.3 collective-permute-start.6
  204.9 4.5 %collective-permute-start.5 = (f32[2,1,32,128]{3,2,1,0:T(8,128)S(1)}, f32[2,1,32,128]{3,2,1,0:T(8,128)S(1)}, u32[]{:S(2)}, u32[]{:S(2)}) collective-permute-start(f32[2,1,32,128]{3,2,1,0:T(8,128)S(1)} %get-tuple-element.82), channel_id=1, source_target_pairs={{0,2},{2,4},{4,6},{1,3},{3,5},{5,7},{8,10},{10,12},{12,14},{9,11},... | collective-permute-start | bytes 98312 | tf_op jit(solution)/shard_map/ppermute | solution.py:25
  209.5 1.6 collective-permute-done.5
  211.1 1.3 collective-permute-start.8
  212.4 3.0 %collective-permute-start.7 = (f32[2,10,1,128]{3,2,1,0:T(1,128)S(1)}, f32[2,10,1,128]{3,2,1,0:T(1,128)S(1)}, u32[]{:S(2)}, u32[]{:S(2)}) collective-permute-start(f32[2,10,1,128]{3,2,1,0:T(1,128)S(1)} %get-tuple-element.73), channel_id=1, source_target_pairs={{0,1},{2,3},{4,5},{6,7},{8,9},{10,11},{12,13},{14,15},{16,17},{18,... | collective-permute-start | bytes 30728 | tf_op jit(solution)/shard_map/ppermute | solution.py:25
  216.3 4.2 %collective-permute-start.9 = (f32[2,10,34,128]{3,2,1,0:T(8,128)S(1)}, f32[2,10,34,128]{3,2,1,0:T(8,128)S(1)}, u32[]{:S(2)}, u32[]{:S(2)}) collective-permute-start(f32[2,10,34,128]{3,2,1,0:T(8,128)S(1)} %pad_maximum_fusion.20), channel_id=1, source_target_pairs={{0,8},{8,16},{16,24},{1,9},{9,17},{17,25},{2,10},{10,18},{18,26},{... | collective-permute-start | bytes 1044488 | tf_op jit(solution)/shard_map/ppermute | solution.py:15
  221.0 8.7 %collective-permute-done.9 = f32[2,10,34,128]{3,2,1,0:T(8,128)S(1)} collective-permute-done((f32[2,10,34,128]{3,2,1,0:T(8,128)S(1)}, f32[2,10,34,128]{3,2,1,0:T(8,128)S(1)}, u32[]{:S(2)}, u32[]{:S(2)}) %collective-permute-start.9) | collective-permute-done | bytes 348192 | tf_op jit(solution)/shard_map/ppermute | solution.py:15
  230.4 0.8 fusion.22
  231.3 0.8 convolution_add_fusion.7
  232.2 0.8 convolution_add_fusion.6
  233.0 0.8 convolution_add_fusion.5
  233.9 0.8 convolution_add_fusion.4
  234.8 0.8 convolution_add_fusion.3
  235.7 0.8 convolution_add_fusion.2
  (81 shorter events, 12.8 us)
Async XLA Ops:
  86.1 5.9 %collective-permute-start.1 = (f32[2,1,32,128]{3,2,1,0:T(8,128)S(1)}, f32[2,1,32,128]{3,2,1,0:T(8,128)S(1)}, u32[]{:S(2)}, u32[]{:S(2)}) collective-permute-start(f32[2,1,32,128]{3,2,1,0:T(8,128)S(1)} %get-tuple-element.88), channel_id=1, source_target_pairs={{2,0},{4,2},{6,4},{3,1},{5,3},{7,5},{10,8},{12,10},{14,12},{11,9},... | collective-permute-start | bytes 98312 | tf_op jit(solution)/shard_map/ppermute | solution.py:26
  87.4 6.1 %collective-permute-start = (f32[2,1,32,128]{3,2,1,0:T(8,128)S(1)}, f32[2,1,32,128]{3,2,1,0:T(8,128)S(1)}, u32[]{:S(2)}, u32[]{:S(2)}) collective-permute-start(f32[2,1,32,128]{3,2,1,0:T(8,128)S(1)} %get-tuple-element.87), channel_id=1, source_target_pairs={{0,2},{2,4},{4,6},{1,3},{3,5},{5,7},{8,10},{10,12},{12,14},{9,11},... | collective-permute-start | bytes 98312 | tf_op jit(solution)/shard_map/ppermute | solution.py:25
  93.6 6.0 %collective-permute-start.3 = (f32[2,10,1,128]{3,2,1,0:T(1,128)S(1)}, f32[2,10,1,128]{3,2,1,0:T(1,128)S(1)}, u32[]{:S(2)}, u32[]{:S(2)}) collective-permute-start(f32[2,10,1,128]{3,2,1,0:T(1,128)S(1)} %get-tuple-element.78), channel_id=1, source_target_pairs={{1,0},{3,2},{5,4},{7,6},{9,8},{11,10},{13,12},{15,14},{17,16},{19,... | collective-permute-start | bytes 30728 | tf_op jit(solution)/shard_map/ppermute | solution.py:26
  94.9 4.7 %collective-permute-start.2 = (f32[2,10,1,128]{3,2,1,0:T(1,128)S(1)}, f32[2,10,1,128]{3,2,1,0:T(1,128)S(1)}, u32[]{:S(2)}, u32[]{:S(2)}) collective-permute-start(f32[2,10,1,128]{3,2,1,0:T(1,128)S(1)} %get-tuple-element.77), channel_id=1, source_target_pairs={{0,1},{2,3},{4,5},{6,7},{8,9},{10,11},{12,13},{14,15},{16,17},{18,... | collective-permute-start | bytes 30728 | tf_op jit(solution)/shard_map/ppermute | solution.py:25
  99.7 12.5 %collective-permute-start.4 = (f32[2,10,34,128]{3,2,1,0:T(8,128)S(1)}, f32[2,10,34,128]{3,2,1,0:T(8,128)S(1)}, u32[]{:S(2)}, u32[]{:S(2)}) collective-permute-start(f32[2,10,34,128]{3,2,1,0:T(8,128)S(1)} %pad_maximum_fusion.18), channel_id=1, source_target_pairs={{0,8},{8,16},{16,24},{1,9},{9,17},{17,25},{2,10},{10,18},{18,26},{... | collective-permute-start | bytes 1044488 | tf_op jit(solution)/shard_map/ppermute | solution.py:15
  119.0 84.5 %copy-start.2 = (f32[128]{0:T(128)S(1)}, f32[128]{0:T(128)}, u32[]{:S(2)}) copy-start(f32[128]{0:T(128)} %param.13) | copy-start | bytes 1540
  119.0 84.5 %copy-start.3 = (f32[128]{0:T(128)S(1)}, f32[128]{0:T(128)}, u32[]{:S(2)}) copy-start(f32[128]{0:T(128)} %param.12) | copy-start | bytes 1540
  119.8 95.6 %copy-start.1 = (f32[3,3,3,128,128]{4,3,2,1,0:T(8,128)S(1)}, f32[3,3,3,128,128]{4,3,2,1,0:T(8,128)}, u32[]{:S(2)}) copy-start(f32[3,3,3,128,128]{4,3,2,1,0:T(8,128)} %param.14) | copy-start | bytes 5308420
  203.6 5.9 %collective-permute-start.6 = (f32[2,1,32,128]{3,2,1,0:T(8,128)S(1)}, f32[2,1,32,128]{3,2,1,0:T(8,128)S(1)}, u32[]{:S(2)}, u32[]{:S(2)}) collective-permute-start(f32[2,1,32,128]{3,2,1,0:T(8,128)S(1)} %get-tuple-element.83), channel_id=1, source_target_pairs={{2,0},{4,2},{6,4},{3,1},{5,3},{7,5},{10,8},{12,10},{14,12},{11,9},... | collective-permute-start | bytes 98312 | tf_op jit(solution)/shard_map/ppermute | solution.py:26
  204.9 6.1 %collective-permute-start.5 = (f32[2,1,32,128]{3,2,1,0:T(8,128)S(1)}, f32[2,1,32,128]{3,2,1,0:T(8,128)S(1)}, u32[]{:S(2)}, u32[]{:S(2)}) collective-permute-start(f32[2,1,32,128]{3,2,1,0:T(8,128)S(1)} %get-tuple-element.82), channel_id=1, source_target_pairs={{0,2},{2,4},{4,6},{1,3},{3,5},{5,7},{8,10},{10,12},{12,14},{9,11},... | collective-permute-start | bytes 98312 | tf_op jit(solution)/shard_map/ppermute | solution.py:25
  211.1 4.5 %collective-permute-start.8 = (f32[2,10,1,128]{3,2,1,0:T(1,128)S(1)}, f32[2,10,1,128]{3,2,1,0:T(1,128)S(1)}, u32[]{:S(2)}, u32[]{:S(2)}) collective-permute-start(f32[2,10,1,128]{3,2,1,0:T(1,128)S(1)} %get-tuple-element.74), channel_id=1, source_target_pairs={{1,0},{3,2},{5,4},{7,6},{9,8},{11,10},{13,12},{15,14},{17,16},{19,... | collective-permute-start | bytes 30728 | tf_op jit(solution)/shard_map/ppermute | solution.py:26
  212.4 3.8 %collective-permute-start.7 = (f32[2,10,1,128]{3,2,1,0:T(1,128)S(1)}, f32[2,10,1,128]{3,2,1,0:T(1,128)S(1)}, u32[]{:S(2)}, u32[]{:S(2)}) collective-permute-start(f32[2,10,1,128]{3,2,1,0:T(1,128)S(1)} %get-tuple-element.73), channel_id=1, source_target_pairs={{0,1},{2,3},{4,5},{6,7},{8,9},{10,11},{12,13},{14,15},{16,17},{18,... | collective-permute-start | bytes 30728 | tf_op jit(solution)/shard_map/ppermute | solution.py:25
  216.3 13.4 %collective-permute-start.9 = (f32[2,10,34,128]{3,2,1,0:T(8,128)S(1)}, f32[2,10,34,128]{3,2,1,0:T(8,128)S(1)}, u32[]{:S(2)}, u32[]{:S(2)}) collective-permute-start(f32[2,10,34,128]{3,2,1,0:T(8,128)S(1)} %pad_maximum_fusion.20), channel_id=1, source_target_pairs={{0,8},{8,16},{16,24},{1,9},{9,17},{17,25},{2,10},{10,18},{18,26},{... | collective-permute-start | bytes 1044488 | tf_op jit(solution)/shard_map/ppermute | solution.py:15
  236.5 1.7 copy-start
  236.5 1.7 copy-start.4
where the time goes:
time: 241 us; the launch traced here: 239 us
  blocking collectives  164 us (68%)
  starting transfers between devices  28.7 us (12%)
  waiting for transfers between devices  20.4 us (8%)
  matrix products  14.8 us (6%)
  other arithmetic  6.13 us (3%)
  local copies, waits for them, and re-layouts  4.27 us (2%)
    psum x2, blocking collectives, group_stats(): lax.psum(jnp.sum(flattened, axis=(0, 2)), ('tm', 'row', 'col'))  84.1 us
    psum x2, blocking collectives, group_stats(): lax.psum(jnp.sum(centered * centered, axis=(0, 2)), ('tm', 'row', 'col'))  80 us
    ppermute x2, waiting for transfers between devices, shifted(): lax.ppermute(value, axis, [(source, source + steps) for source in range(f...  16.5 us
    ppermute x4, starting transfers between devices, padded_2(): before = lax.ppermute(last, axis, up)  15.2 us
    dot_general x18, matrix products, conv_valid(): jnp.dot(slab.reshape(-1, 3 * channels), weights[time_tap, row_tap].reshap...  14.8 us
    ppermute x2, starting transfers between devices, shifted(): lax.ppermute(value, axis, [(source, source + steps) for source in range(f...  8.41 us
    ppermute x4, starting transfers between devices, padded_2(): after = lax.ppermute(first, axis, down)  5.17 us
  transfers between devices with their start and end apart: 10, of which 5 were waited for; matrix products, arithmetic and copies ran while one was open for 1% of the time, Pallas kernels for 0%

commit v1 on v0

v1 whole, which is shorter than its diff:
```python
import functools
import jax
import jax.numpy as jnp
from jax import lax
from jax.experimental import pallas as pl
from jax.experimental.pallas import tpu as pltpu
from jax.sharding import PartitionSpec as P

GROUPS = 32
MESH = pl.DeviceIdType.MESH
epsilon = 1e-06
F32 = jnp.float32
BF16 = jnp.bfloat16
STEPS = [
    (ahead, down, right)
    for ahead in (0, 1)
    for down in (-1, 0, 1)
    for right in (-1, 0, 1)
    if (ahead, down, right) != (0, 0, 0)
]


def repeat(count, body):
    if count <= 8:
        for i in range(count):
            body(i)
    else:
        lax.fori_loop(0, count, lambda i, _: (body(i), 0)[1], 0)


def group_total(value):
    channels = value.shape[-1]
    lane = lax.broadcasted_iota(jnp.int32, value.shape, 1)
    step = 1
    while step < channels // GROUPS:
        upper = pltpu.roll(value, channels - step, 1)
        lower = pltpu.roll(value, step, 1)
        value = value + jnp.where((lane & step) == 0, upper, lower)
        step *= 2
    return value


def split(value):
    high = value.astype(BF16)
    return high, (value - high.astype(F32)).astype(BF16)


def kernel(
    counts,
    feat_hbm, gain1, shift1, w1_hbm, gain2, shift2, w2_hbm, bias,
    out_ref,
    x_ref, hid_ref, w_raw, w_split, high, low, part,
    edge_cols, corners, front, got_rows, got_cols, got_corners, stat_a, stat_b,
    load_sem, halo_send, halo_recv, a_send, a_recv, b_send, b_recv,
):
    n_tm, n_row, n_col = counts
    n_rc = n_row * n_col
    tm, row, col = lax.axis_index("tm"), lax.axis_index("row"), lax.axis_index("col")
    rc = row * n_col + col
    frames, height, width, channels = x_ref.shape
    cells = frames * height * width
    per_group = channels // GROUPS
    taps = 9 * channels

    def exists(ahead, down, right):
        ok = (row + down >= 0) & (row + down < n_row)
        ok = ok & (col + right >= 0) & (col + right < n_col)
        return ok & (tm + ahead >= 0) & (tm + ahead < n_tm)

    feat_load = pltpu.make_async_copy(feat_hbm, x_ref, load_sem.at[0])
    feat_load.start()
    w_load = [
        pltpu.make_async_copy(w_hbm, w_raw.at[layer], load_sem.at[1 + layer])
        for layer, w_hbm in enumerate((w1_hbm, w2_hbm))
    ]
    for load in w_load:
        load.start()

    barrier = pltpu.get_barrier_semaphore()
    expected = jnp.int32(n_rc - 1 + n_tm - 1)

    def greet_rc(i):
        other = lax.rem(rc + 1 + i, n_rc)
        pl.semaphore_signal(
            barrier, inc=1, device_id=(tm, other // n_col, lax.rem(other, n_col)), device_id_type=MESH
        )

    def greet_tm(i):
        pl.semaphore_signal(
            barrier, inc=1, device_id=(lax.rem(tm + 1 + i, n_tm), row, col), device_id_type=MESH
        )

    repeat(n_rc - 1, greet_rc)
    repeat(n_tm - 1, greet_tm)
    for ahead in (-1, 1):
        for down in (-1, 0, 1):
            for right in (-1, 0, 1):
                if (down, right) == (0, 0):
                    continue
                here = exists(ahead, down, right)
                expected = expected + here.astype(jnp.int32)

                @pl.when(here)
                def _():
                    pl.semaphore_signal(
                        barrier, inc=1, device_id=(tm + ahead, row + down, col + right), device_id_type=MESH
                    )

    def halo_copy(layer, source, k):
        ahead, down, right = STEPS[k]
        if (down, right) == (0, 0):
            src, dst = source, front.at[layer]
        elif right == 0:
            side = (1 - down) // 2
            src = source.at[:, height - 1 if down == 1 else 0]
            dst = got_rows.at[layer, ahead, side]
        elif down == 0:
            side = (1 - right) // 2
            src = edge_cols.at[layer, side]
            dst = got_cols.at[layer, ahead, side]
        else:
            r_side, c_side = (1 - down) // 2, (1 - right) // 2
            src = corners.at[layer, r_side, c_side]
            dst = got_corners.at[layer, ahead, r_side, c_side]
        return pltpu.make_async_remote_copy(
            src_ref=src,
            dst_ref=dst,
            send_sem=halo_send.at[layer, k],
            recv_sem=halo_recv.at[layer, k],
            device_id=(tm + ahead, row + down, col + right),
            device_id_type=MESH,
        )

    def for_sends(layer, source, act, chosen=lambda step: True):
        for k, step in enumerate(STEPS):
            if chosen(step):

                @pl.when(exists(*step))
                def _():
                    act(halo_copy(layer, source, k))

    def wait_halo(layer, source, ahead):
        for k, step in enumerate(STEPS):
            if step[0] == ahead:

                @pl.when(exists(-step[0], -step[1], -step[2]))
                def _():
                    halo_copy(layer, source, k).wait_recv()

    def pack_edges(layer, source):
        for r_side in range(2):
            for c_side in range(2):
                corners[layer, r_side, c_side] = jnp.zeros((8, channels), F32)
        for frame in range(frames):
            for c_side, w in ((0, width - 1), (1, 0)):
                for h in range(height):
                    line = source[frame, h, w : w + 1, :]
                    edge_cols[layer, c_side, frame, h : h + 1, :] = line
                    if h in (0, height - 1):
                        corners[layer, 0 if h else 1, c_side, frame : frame + 1, :] = line

    def a_copy(layer, i):
        other = lax.rem(rc + 1 + i, n_rc)
        return pltpu.make_async_remote_copy(
            src_ref=stat_a.at[layer, rc],
            dst_ref=stat_a.at[layer, rc],
            send_sem=a_send.at[layer, i],
            recv_sem=a_recv.at[layer, rc],
            device_id=(tm, other // n_col, lax.rem(other, n_col)),
            device_id_type=MESH,
        )

    def a_wait(layer, i):
        other = lax.rem(rc + 1 + i, n_rc)
        pltpu.make_async_remote_copy(
            src_ref=stat_a.at[layer, other],
            dst_ref=stat_a.at[layer, other],
            send_sem=a_send.at[layer, i],
            recv_sem=a_recv.at[layer, other],
            device_id=(tm, other // n_col, lax.rem(other, n_col)),
            device_id_type=MESH,
        ).wait_recv()

    def b_copy(layer, i):
        return pltpu.make_async_remote_copy(
            src_ref=stat_b.at[layer, tm],
            dst_ref=stat_b.at[layer, tm],
            send_sem=b_send.at[layer, i],
            recv_sem=b_recv.at[layer, tm],
            device_id=(lax.rem(tm + 1 + i, n_tm), row, col),
            device_id_type=MESH,
        )

    def b_wait(layer, i):
        other = lax.rem(tm + 1 + i, n_tm)
        pltpu.make_async_remote_copy(
            src_ref=stat_b.at[layer, other],
            dst_ref=stat_b.at[layer, other],
            send_sem=b_send.at[layer, i],
            recv_sem=b_recv.at[layer, other],
            device_id=(other, row, col),
            device_id_type=MESH,
        ).wait_recv()

    tile_row = lax.broadcasted_iota(jnp.int32, (8, channels), 0)

    def tile(mean, spread):
        return jnp.where(tile_row == 0, mean, jnp.where(tile_row == 1, spread, 0.0))

    def local_stats(layer, source):
        values = source[...].reshape(cells, channels)
        mean = jnp.sum(values, axis=0, keepdims=True) * (1.0 / cells)
        centered = values - mean
        stat_a[layer, rc] = tile(mean, jnp.sum(centered * centered, axis=0, keepdims=True))

    def joined(block, entry_count, per_lane):
        shares = block.shape[0]
        total = jnp.sum(block, axis=0)
        center = jnp.broadcast_to(total[0:1], (8, channels))
        center = group_total(center) * (1.0 / (shares * per_group)) if per_lane else center * (1.0 / shares)
        away = block - center[None]
        away = jnp.sum(away * away, axis=0)
        spread = jnp.broadcast_to(total[1:2] + entry_count * away[0:1], (8, channels))
        return center, (group_total(spread) if per_lane else spread)

    def convert(layer):
        w_load[layer].wait()
        piece = channels

        def body(i, _):
            at = pl.ds(pl.multiple_of(i * piece, piece), piece)
            for dt in range(3):
                w_high, w_low = split(w_raw[layer, dt, at, :])
                w_split[layer, dt, at, 0:channels] = w_high
                w_split[layer, dt, at, channels:] = w_low
            return 0

        lax.fori_loop(0, 9, body, 0)

    column = lax.broadcasted_iota(jnp.int32, (height, width, channels), 1)

    def store_taps(frame, first, value, left, right):
        rows = value.shape[0]
        at = column[:rows]
        before = jnp.where(at == 0, left[:, None, :], pltpu.roll(value, 1, 1))
        after = jnp.where(at == width - 1, right[:, None, :], pltpu.roll(value, width - 1, 1))
        for j, shifted in enumerate((before, value, after)):
            v_high, v_low = split(shifted)
            high[frame, first : first + rows, :, j * channels : (j + 1) * channels] = v_high
            low[frame, first : first + rows, :, j * channels : (j + 1) * channels] = v_low

    def spread_frame(layer, source, ahead, frame, activate):
        to = frame + frames * (1 - ahead)

        def valid(down, right, value):
            return jnp.where(exists(-ahead, -down, -right), value, 0.0)

        left = valid(0, 1, activate(got_cols[layer, ahead, 0, frame]))
        right = valid(0, -1, activate(got_cols[layer, ahead, 1, frame]))
        store_taps(to, 1, activate(source[frame]), left, right)
        for side, down in ((0, 1), (1, -1)):
            line = valid(down, 0, activate(got_rows[layer, ahead, side, frame]))
            left = valid(down, 1, activate(got_corners[layer, ahead, side, 0, frame : frame + 1]))
            right = valid(down, -1, activate(got_corners[layer, ahead, side, 1, frame : frame + 1]))
            store_taps(to, 0 if side == 0 else height + 1, line[None], left, right)

    def lines(array, frame):
        return jnp.concatenate(
            [array[frame, dh : dh + height].reshape(height * width, 3 * channels) for dh in range(3)], axis=1
        )

    def dot(a, b):
        return jnp.dot(a, b, preferred_element_type=F32)

    def fold(value):
        return value[:, :channels] + value[:, channels:]

    def conv_half(layer, near, pair, far, dt_near_first):
        w = [w_split.at[layer, dt] for dt in range(3)]
        h_pair, l_pair = lines(high, pair), lines(low, pair)
        h_far, l_far = lines(high, far), lines(low, far)
        first, second = (2, 1) if near else (1, 0)
        only = 2 if near else 0
        both = dot(l_pair, jnp.concatenate([w[first][:, :channels], w[second][:, :channels]], axis=1))
        out_first = fold(dot(h_pair, w[first][...])) + both[:, :channels]
        out_second = fold(dot(h_pair, w[second][...])) + both[:, channels:]
        rest = fold(dot(h_far, w[only][...])) + dot(l_far, w[only][:, :channels])
        if near:
            return out_first, out_second + rest
        return out_first + rest, out_second

    pair_cells = height * width

    def layer_pass(layer, source, gain, shift, before_stats):
        local_stats(layer, source)
        pack_edges(layer, source)
        before_stats()
        repeat(n_rc - 1, lambda i: a_copy(layer, i).start())
        for_sends(layer, source, lambda c: c.start(), lambda s: s[0] == 0)
        for_sends(layer, source, lambda c: c.start(), lambda s: s[0] == 1)
        convert(layer)
        repeat(n_rc - 1, lambda i: a_wait(layer, i))
        center, spread = joined(stat_a[layer], float(cells), True)
        stat_b[layer, tm] = tile(center[0:1], spread[0:1])
        repeat(n_tm - 1, lambda i: b_copy(layer, i).start())
        repeat(n_tm - 1, lambda i: b_wait(layer, i))
        each = float(cells * n_rc * per_group)
        center, spread = joined(stat_b[layer], each, False)
        center = center[0:1]
        scale = lax.rsqrt(spread[0:1] * (1.0 / (each * n_tm)) + epsilon)

        def activate(value):
            lead = (1,) * (value.ndim - 2) + (1, channels)
            u = (value - center.reshape(lead)) * scale.reshape(lead) * gain[...].reshape(lead)
            u = u + shift[...].reshape(lead)
            return u / (1.0 + jnp.exp(-u))

        wait_halo(layer, source, 0)
        for frame in range(frames):
            spread_frame(layer, source, 0, frame, activate)
        first, second = conv_half(layer, True, 2, 3, None)
        part[0], part[1] = first, second

        wait_halo(layer, source, 1)

        @pl.when(tm == 0)
        def _():
            for to in range(2):
                high[to] = high[2]
                low[to] = low[2]

        @pl.when(tm != 0)
        def _():
            for frame in range(frames):
                spread_frame(layer, front.at[layer], 1, frame, activate)

        first, second = conv_half(layer, False, 1, 0, None)
        return part[0] + first, part[1] + second

    feat_load.wait()
    pair = layer_pass(0, x_ref, gain1, shift1, lambda: pl.semaphore_wait(barrier, expected))
    for frame in range(frames):
        hid_ref[frame] = pair[frame].reshape(height, width, channels)
    pair = layer_pass(1, hid_ref, gain2, shift2, lambda: None)
    for frame in range(frames):
        moved = pair[frame].reshape(height, width, channels)
        out_ref[frame] = x_ref[frame] + moved + bias[...].reshape(1, 1, channels)

    for layer, source in enumerate((x_ref, hid_ref)):
        repeat(n_rc - 1, lambda i: a_copy(layer, i).wait_send())
        repeat(n_tm - 1, lambda i: b_copy(layer, i).wait_send())
        for_sends(layer, source, lambda c: c.wait_send())


def local(counts, features, gain1, shift1, weight1, gain2, shift2, weight2, bias):
    n_tm, n_row, n_col = counts
    frames, height, width, channels = features.shape
    taps = 9 * channels
    n_rc = n_row * n_col
    lane = lambda v: v.reshape(1, channels)
    weights = lambda w: w.reshape(3, taps, channels)
    vmem = pl.BlockSpec(memory_space=pltpu.VMEM)
    hbm = pl.BlockSpec(memory_space=pl.ANY)
    padded = (2 * frames, height + 2, width, 3 * channels)
    dma = pltpu.SemaphoreType.DMA
    return pl.pallas_call(
        functools.partial(kernel, counts),
        out_shape=jax.ShapeDtypeStruct(features.shape, F32),
        in_specs=[hbm, vmem, vmem, hbm, vmem, vmem, hbm, vmem],
        out_specs=vmem,
        scratch_shapes=[
            pltpu.VMEM(features.shape, F32),
            pltpu.VMEM(features.shape, F32),
            pltpu.VMEM((2, 3, taps, channels), F32),
            pltpu.VMEM((2, 3, taps, 2 * channels), BF16),
            pltpu.VMEM(padded, BF16),
            pltpu.VMEM(padded, BF16),
            pltpu.VMEM((2, height * width, channels), F32),
            pltpu.VMEM((2, 2, frames, height, channels), F32),
            pltpu.VMEM((2, 2, 2, 8, channels), F32),
            pltpu.VMEM((2, *features.shape), F32),
            pltpu.VMEM((2, 2, 2, frames, width, channels), F32),
            pltpu.VMEM((2, 2, 2, frames, height, channels), F32),
            pltpu.VMEM((2, 2, 2, 2, 8, channels), F32),
            pltpu.VMEM((2, n_rc, 8, channels), F32),
            pltpu.VMEM((2, n_tm, 8, channels), F32),
            dma((3,)),
            dma((2, len(STEPS))),
            dma((2, len(STEPS))),
            dma((2, max(1, n_rc - 1))),
            dma((2, n_rc)),
            dma((2, max(1, n_tm - 1))),
            dma((2, n_tm)),
        ],
        compiler_params=pltpu.CompilerParams(
            collective_id=0, has_side_effects=True, vmem_limit_bytes=40 * 1024 * 1024
        ),
    )(features, lane(gain1), lane(shift1), weights(weight1), lane(gain2), lane(shift2), weights(weight2), lane(bias))


def solution(mesh):
    counts = tuple(mesh.shape[axis] for axis in ("tm", "row", "col"))
    in_specs = (P("tm", "row", "col", None), P(), P(), P(), P(), P(), P(), P())
    out_specs = P("tm", "row", "col", None)
    return jax.shard_map(
        functools.partial(local, counts), mesh=mesh, in_specs=in_specs, out_specs=out_specs, check_vma=False
    )
```

time: 241 us -> 37.8 us (0.16)
  blocking collectives: 164 us -> 0 us
  Pallas kernels: 0 us -> 29.7 us
  starting transfers between devices: 28.7 us -> 0 us
  waiting for transfers between devices: 20.4 us -> 0 us
  matrix products: 14.8 us -> 0 us
  other arithmetic: 6.13 us -> 0 us
  local copies, waits for them, and re-layouts: 4.27 us -> 7.88 us
    psum x4 -> x0, blocking collectives: 164 us -> none  [the longest x2 84.1 us: group_stats(): lax.psum(jnp.sum(flattened, axis=(0, 2)), ('tm', 'row', 'col'))]
    pallas_call x0 -> x1, Pallas kernels: none -> 29.7 us  [local(): pl.pallas_call(functools.partial(kernel, counts), out_shape=jax.ShapeDtyp...]
    ppermute x10 -> x0, starting transfers between devices: 28.7 us -> none  [the longest x4 15.2 us: padded_2(): before = lax.ppermute(last, axis, up)]
    ppermute x10 -> x0, waiting for transfers between devices: 20.4 us -> none  [the longest x2 16.5 us: shifted(): lax.ppermute(value, axis, [(source, source + steps) for source in range(f...]
    dot_general x18 -> x0, matrix products: 14.8 us -> none  [conv_valid(): jnp.dot(slab.reshape(-1, 3 * channels), weights[time_tap, row_tap].reshap...]
    unnamed x10 -> x17, local copies, waits for them, and re-layouts: 0.03 us -> 7.88 us
    slice x13 -> x0, local copies, waits for them, and re-layouts: 3.13 us -> none  [the longest x2 1.75 us: conv_valid(): weights[time_tap, row_tap].reshape(3 * channels, -1)]
    reduce_sum x7 -> x0, other arithmetic: 2.61 us -> none  [the longest x4 1.35 us: group_stats(): jnp.sum(centered * centered, axis=(0, 2))]
  transfers between devices with their start and end apart: 10 -> 0, of which waited for: 5 -> 0; matrix products, arithmetic and copies ran while one was open for 1% -> 0% of each run, Pallas kernels for 0% -> 0%
where the time goes in v1:
time: 37.8 us; the launch traced here: 37.6 us
  Pallas kernels  29.7 us (79%)
  local copies, waits for them, and re-layouts  7.88 us (21%)
    pallas_call x1, Pallas kernels, local(): pl.pallas_call(functools.partial(kernel, counts), out_shape=jax.ShapeDtyp...  29.7 us
    unnamed x17, local copies, waits for them, and re-layouts  7.88 us

profile of v1, /device:TPU:0, one launch (start us, length us, event | category | flops | bytes accessed | tf_op | source)
XLA Modules:
  0.0 37.6 jit_solution(5880481412934246166)
XLA Ops:
  0.0 0.0 copy-start
  0.0 1.5 %copy-done = f32[3,3,3,128,128]{4,3,2,1,0:T(8,128)S(1)} copy-done((f32[3,3,3,128,128]{4,3,2,1,0:T(8,128)S(1)}, f32[3,3,3,128,128]{4,3,2,1,0:T(8,128)}, u32[]{:S(2)}) %copy-start) | copy-done | bytes 1769496
  1.5 0.0 copy-start.1
  1.5 1.5 %copy-done.1 = f32[3,3,3,128,128]{4,3,2,1,0:T(8,128)S(1)} copy-done((f32[3,3,3,128,128]{4,3,2,1,0:T(8,128)S(1)}, f32[3,3,3,128,128]{4,3,2,1,0:T(8,128)}, u32[]{:S(2)}) %copy-start.1) | copy-done | bytes 1769496
  3.0 0.0 copy-start.2
  3.0 0.9 %copy-done.2 = f32[2,8,32,128]{3,2,1,0:T(8,128)S(1)} copy-done((f32[2,8,32,128]{3,2,1,0:T(8,128)S(1)}, f32[2,8,32,128]{3,2,1,0:T(8,128)}, u32[]{:S(2)}) %copy-start.2) | copy-done | bytes 262168
  3.9 0.0 copy-start.3
  3.9 0.7 %copy-done.3 = f32[128]{0:T(128)S(1)} copy-done((f32[128]{0:T(128)S(1)}, f32[128]{0:T(128)}, u32[]{:S(2)}) %copy-start.3) | copy-done | bytes 536
  4.6 0.0 copy-start.4
  4.6 0.7 %copy-done.4 = f32[128]{0:T(128)S(1)} copy-done((f32[128]{0:T(128)S(1)}, f32[128]{0:T(128)}, u32[]{:S(2)}) %copy-start.4) | copy-done | bytes 536
  5.2 0.0 copy-start.5
  5.2 0.7 %copy-done.5 = f32[128]{0:T(128)S(1)} copy-done((f32[128]{0:T(128)S(1)}, f32[128]{0:T(128)}, u32[]{:S(2)}) %copy-start.5) | copy-done | bytes 536
  5.9 0.0 copy-start.6
  5.9 0.7 %copy-done.6 = f32[128]{0:T(128)S(1)} copy-done((f32[128]{0:T(128)S(1)}, f32[128]{0:T(128)}, u32[]{:S(2)}) %copy-start.6) | copy-done | bytes 536
  6.5 0.0 copy-start.7
  6.5 0.7 %copy-done.7 = f32[128]{0:T(128)S(1)} copy-done((f32[128]{0:T(128)S(1)}, f32[128]{0:T(128)}, u32[]{:S(2)}) %copy-start.7) | copy-done | bytes 536
  7.2 29.7 %shard_map.82 = f32[2,8,32,128]{3,2,1,0:T(8,128)S(1)} custom-call(f32[2,8,32,128]{3,2,1,0:T(8,128)S(1)} %copy-done.2, f32[1,128]{1,0:T(1,128)S(1)} %bitcast.9, f32[1,128]{1,0:T(1,128)S(1)} %bitcast.10, f32[3,1152,128]{2,1,0:T(8,128)S(1)} %bitcast.7, f32[1,128]{1,0:T(1,128)S(1)} %bitcast.11, f32[1,128]{1,0:T(1,128)S(1)} %bitcast.12, ...), custom_call_target="tpu_custom_call" | custom-call | tf_op jit(solution)/shard_map/pallas_call | solution.py:366
  36.9 0.7 %copy.10 = f32[2,8,32,128]{3,2,1,0:T(8,128)} copy(f32[2,8,32,128]{3,2,1,0:T(8,128)S(1)} %shard_map.82) | data formatting | bytes 524288
Async XLA Ops:
  0.0 1.5 %copy-start = (f32[3,3,3,128,128]{4,3,2,1,0:T(8,128)S(1)}, f32[3,3,3,128,128]{4,3,2,1,0:T(8,128)}, u32[]{:S(2)}) copy-start(f32[3,3,3,128,128]{4,3,2,1,0:T(8,128)} %param.11) | copy-start | bytes 5308420
  1.5 1.5 %copy-start.1 = (f32[3,3,3,128,128]{4,3,2,1,0:T(8,128)S(1)}, f32[3,3,3,128,128]{4,3,2,1,0:T(8,128)}, u32[]{:S(2)}) copy-start(f32[3,3,3,128,128]{4,3,2,1,0:T(8,128)} %param.14) | copy-start | bytes 5308420
  3.0 0.9 %copy-start.2 = (f32[2,8,32,128]{3,2,1,0:T(8,128)S(1)}, f32[2,8,32,128]{3,2,1,0:T(8,128)}, u32[]{:S(2)}) copy-start(f32[2,8,32,128]{3,2,1,0:T(8,128)} %feat_hbm.1) | copy-start | bytes 786436
  3.9 0.7 %copy-start.3 = (f32[128]{0:T(128)S(1)}, f32[128]{0:T(128)}, u32[]{:S(2)}) copy-start(f32[128]{0:T(128)} %param.9) | copy-start | bytes 1540
  4.6 0.7 %copy-start.4 = (f32[128]{0:T(128)S(1)}, f32[128]{0:T(128)}, u32[]{:S(2)}) copy-start(f32[128]{0:T(128)} %param.10) | copy-start | bytes 1540
  5.2 0.7 %copy-start.5 = (f32[128]{0:T(128)S(1)}, f32[128]{0:T(128)}, u32[]{:S(2)}) copy-start(f32[128]{0:T(128)} %param.12) | copy-start | bytes 1540
  5.9 0.7 %copy-start.6 = (f32[128]{0:T(128)S(1)}, f32[128]{0:T(128)}, u32[]{:S(2)}) copy-start(f32[128]{0:T(128)} %param.13) | copy-start | bytes 1540
  6.5 0.7 %copy-start.7 = (f32[128]{0:T(128)S(1)}, f32[128]{0:T(128)}, u32[]{:S(2)}) copy-start(f32[128]{0:T(128)} %param.15) | copy-start | bytes 1540

commit v2 on v1

v2 whole, which is shorter than its diff:
```python
import functools
import jax
import jax.numpy as jnp
from jax import lax
from jax.experimental import pallas as pl
from jax.experimental.pallas import tpu as pltpu
from jax.sharding import PartitionSpec as P

GROUPS = 32
MESH = pl.DeviceIdType.MESH
epsilon = 1e-06
F32 = jnp.float32
BF16 = jnp.bfloat16
STEPS = [
    (ahead, down, right)
    for ahead in (0, 1)
    for down in (-1, 0, 1)
    for right in (-1, 0, 1)
    if (down, right) != (0, 0)
]


def repeat(count, body):
    if count <= 4:
        for i in range(count):
            body(i)
    else:
        lax.fori_loop(0, count, lambda i, _: (body(i), 0)[1], 0)


def group_total(value):
    channels = value.shape[-1]
    lane = lax.broadcasted_iota(jnp.int32, value.shape, 1)
    step = 1
    while step < channels // GROUPS:
        upper = pltpu.roll(value, channels - step, 1)
        lower = pltpu.roll(value, step, 1)
        value = value + jnp.where((lane & step) == 0, upper, lower)
        step *= 2
    return value


def split(value):
    high = value.astype(BF16)
    return high, (value - high.astype(F32)).astype(BF16)


def kernel(
    counts,
    feat_hbm, gain1_hbm, shift1_hbm, w1_hbm, gain2_hbm, shift2_hbm, w2_hbm, bias_hbm,
    out_ref,
    lanes,
    x_ref, hid_ref, w_raw, w_split, high, low, part,
    edge_cols, corners, front, got_rows, got_cols, got_corners, stats,
    load_sem, halo_send, halo_recv, front_send, front_recv, stat_send, stat_recv,
):
    n_tm, n_row, n_col = counts
    n_all = n_tm * n_row * n_col
    tm, row, col = lax.axis_index("tm"), lax.axis_index("row"), lax.axis_index("col")
    rank = (tm * n_row + row) * n_col + col
    frames, height, width, channels = x_ref.shape
    cells = frames * height * width
    per_group = channels // GROUPS

    def place(index):
        return index // (n_row * n_col), lax.rem(index // n_col, n_row), lax.rem(index, n_col)

    def exists(ahead, down, right):
        ok = (row + down >= 0) & (row + down < n_row)
        ok = ok & (col + right >= 0) & (col + right < n_col)
        return ok & (tm + ahead >= 0) & (tm + ahead < n_tm)

    feat_load = pltpu.make_async_copy(feat_hbm, x_ref, load_sem.at[0])
    feat_load.start()
    w_load = [
        pltpu.make_async_copy(w_hbm, w_raw.at[layer], load_sem.at[1 + layer])
        for layer, w_hbm in enumerate((w1_hbm, w2_hbm))
    ]
    lane_hbm = (gain1_hbm, shift1_hbm, gain2_hbm, shift2_hbm, bias_hbm)
    lane_load = [pltpu.make_async_copy(v, lanes.at[i], load_sem.at[3 + i]) for i, v in enumerate(lane_hbm)]
    gain1, shift1, gain2, shift2, bias = [lanes.at[i] for i in range(5)]
    for load in (*w_load, *lane_load):
        load.start()

    barrier = pltpu.get_barrier_semaphore()

    def greet(i):
        pl.semaphore_signal(
            barrier, inc=1, device_id=place(lax.rem(rank + 1 + i, n_all)), device_id_type=MESH
        )

    repeat(n_all - 1, greet)

    def halo_copy(layer, source, k):
        ahead, down, right = STEPS[k]
        if right == 0:
            side = (1 - down) // 2
            src = source.at[:, height - 1 if down == 1 else 0]
            dst = got_rows.at[layer, ahead, side]
        elif down == 0:
            side = (1 - right) // 2
            src = edge_cols.at[layer, side]
            dst = got_cols.at[layer, ahead, side]
        else:
            r_side, c_side = (1 - down) // 2, (1 - right) // 2
            src = corners.at[layer, r_side, c_side]
            dst = got_corners.at[layer, ahead, r_side, c_side]
        return pltpu.make_async_remote_copy(
            src_ref=src,
            dst_ref=dst,
            send_sem=halo_send.at[layer, k],
            recv_sem=halo_recv.at[layer, k],
            device_id=(tm + ahead, row + down, col + right),
            device_id_type=MESH,
        )

    def front_copy(layer, source, frame):
        return pltpu.make_async_remote_copy(
            src_ref=source.at[frame],
            dst_ref=front.at[layer, frame],
            send_sem=front_send.at[layer, frame],
            recv_sem=front_recv.at[layer, frame],
            device_id=(tm + 1, row, col),
            device_id_type=MESH,
        )

    def send_front(layer, source, frame):
        @pl.when(tm + 1 < n_tm)
        def _():
            front_copy(layer, source, frame).start()

    def for_sends(layer, source, act):
        for k, step in enumerate(STEPS):


            @pl.when(exists(*step))
            def _():
                act(halo_copy(layer, source, k))

    def wait_halo(layer, source, ahead):
        for k, step in enumerate(STEPS):
            if step[0] == ahead:

                @pl.when(exists(-step[0], -step[1], -step[2]))
                def _():
                    halo_copy(layer, source, k).wait_recv()

    def pack_edges(layer, source):
        for r_side in range(2):
            for c_side in range(2):
                corners[layer, r_side, c_side] = jnp.zeros((8, channels), F32)
        for frame in range(frames):
            for c_side, w in ((0, width - 1), (1, 0)):
                for h in range(height):
                    line = source[frame, h, w : w + 1, :]
                    edge_cols[layer, c_side, frame, h : h + 1, :] = line
                    if h in (0, height - 1):
                        corners[layer, 0 if h else 1, c_side, frame : frame + 1, :] = line

    def stat_copy(layer, i):
        to = lax.rem(rank + 1 + i, n_all)
        return pltpu.make_async_remote_copy(
            src_ref=stats.at[layer, rank],
            dst_ref=stats.at[layer, rank],
            send_sem=stat_send.at[layer],
            recv_sem=stat_recv.at[layer],
            device_id=place(to),
            device_id_type=MESH,
        )

    def stat_wait(layer):
        others = stats.at[layer, pl.ds(0, n_all - 1)]
        return pltpu.make_async_remote_copy(
            src_ref=others,
            dst_ref=others,
            send_sem=stat_send.at[layer],
            recv_sem=stat_recv.at[layer],
            device_id=place(lax.rem(rank + 1, n_all)),
            device_id_type=MESH,
        )

    def local_stats(layer, source):
        values = source[...].reshape(cells, channels)
        mean = jnp.sum(values, axis=0, keepdims=True) * (1.0 / cells)
        centered = values - mean
        stats[layer, rank, 0:1] = mean
        stats[layer, rank, 1:2] = jnp.sum(centered * centered, axis=0, keepdims=True)

    def joined(layer):
        block = stats[layer]
        total = jnp.sum(block, axis=0)
        center = jnp.broadcast_to(total[0:1], (8, channels))
        center = group_total(center)[0:1] * (1.0 / (n_all * per_group))
        away = block[:, 0:1, :] - center[None]
        spread = total[1:2] + float(cells) * jnp.sum(away * away, axis=0)
        spread = group_total(jnp.broadcast_to(spread, (8, channels)))[0:1]
        return center, spread * (1.0 / (float(cells) * n_all * per_group))

    def convert(layer):
        w_load[layer].wait()
        piece = channels

        def body(i, _):
            at = pl.ds(pl.multiple_of(i * piece, piece), piece)
            for dt in range(3):
                w_high, w_low = split(w_raw[layer, dt, at, :])
                w_split[layer, dt, at, 0:channels] = w_high
                w_split[layer, dt, at, channels:] = w_low
            return 0

        lax.fori_loop(0, 9, body, 0)

    column = lax.broadcasted_iota(jnp.int32, (height, width, channels), 1)

    def store_taps(frame, first, value, left, right):
        rows = value.shape[0]
        at = column[:rows]
        before = jnp.where(at == 0, left[:, None, :], pltpu.roll(value, 1, 1))
        after = jnp.where(at == width - 1, right[:, None, :], pltpu.roll(value, width - 1, 1))
        for j, shifted in enumerate((before, value, after)):
            v_high, v_low = split(shifted)
            high[frame, first : first + rows, :, j * channels : (j + 1) * channels] = v_high
            low[frame, first : first + rows, :, j * channels : (j + 1) * channels] = v_low

    def spread_frame(layer, source, ahead, frame, activate):
        to = frame + frames * (1 - ahead)

        def valid(down, right, value):
            return jnp.where(exists(-ahead, -down, -right), value, 0.0)

        left = valid(0, 1, activate(got_cols[layer, ahead, 0, frame]))
        right = valid(0, -1, activate(got_cols[layer, ahead, 1, frame]))
        store_taps(to, 1, activate(source[frame]), left, right)
        for side, down in ((0, 1), (1, -1)):
            line = valid(down, 0, activate(got_rows[layer, ahead, side, frame]))
            left = valid(down, 1, activate(got_corners[layer, ahead, side, 0, frame : frame + 1]))
            right = valid(down, -1, activate(got_corners[layer, ahead, side, 1, frame : frame + 1]))
            store_taps(to, 0 if side == 0 else height + 1, line[None], left, right)

    def lines(array, frame):
        return jnp.concatenate(
            [array[frame, dh : dh + height].reshape(height * width, 3 * channels) for dh in range(3)], axis=1
        )

    def dot(a, b):
        return jnp.dot(a, b, preferred_element_type=F32)

    def fold(value):
        return value[:, :channels] + value[:, channels:]

    def conv_pair(layer, frame, near):
        w = [w_split.at[layer, dt] for dt in range(3)]
        first, second = (2, 1) if near else (1, 0)
        h, l = lines(high, frame), lines(low, frame)
        both = dot(l, jnp.concatenate([w[first][:, :channels], w[second][:, :channels]], axis=1))
        out_second = fold(dot(h, w[second][...])) + both[:, channels:]
        return fold(dot(h, w[first][...])) + both[:, :channels], out_second

    def conv_one(layer, frame, dt):
        w = w_split.at[layer, dt]
        return fold(dot(lines(high, frame), w[...])) + dot(lines(low, frame), w[:, :channels])

    def start_stats(layer):
        repeat(n_all - 1, lambda i: stat_copy(layer, i).start())

    def layer_pass(layer, source, gain, shift, beside, emit):
        if layer == 0:
            convert(0)
        stat_wait(layer).wait_recv()
        center, spread = joined(layer)
        scale = lax.rsqrt(spread + epsilon)

        def activate(value):
            lead = (1,) * (value.ndim - 2) + (1, channels)
            u = (value - center.reshape(lead)) * scale.reshape(lead) * gain[...].reshape(lead)
            u = u + shift[...].reshape(lead)
            return u / (1.0 + jnp.exp(-u))

        wait_halo(layer, source, 0)
        for frame in range(frames):
            spread_frame(layer, source, 0, frame, activate)
        part[0], part[1] = conv_pair(layer, 2, True)
        part[1] += conv_one(layer, 3, 2)
        beside()
        wait_halo(layer, source, 1)

        def arrived(frame):
            @pl.when(tm == 0)
            def _():
                high[frame] = high[2]
                low[frame] = low[2]

            @pl.when(tm != 0)
            def _():
                front_copy(layer, source, frame).wait_recv()
                spread_frame(layer, front.at[layer], 1, frame, activate)

        arrived(1)
        first, second = conv_pair(layer, 1, False)
        part[0] += first
        emit(1, part[1] + second)
        arrived(0)
        emit(0, part[0] + conv_one(layer, 0, 0))

    def keep_hidden(frame, value):
        hid_ref[frame] = value.reshape(height, width, channels)
        send_front(1, hid_ref, frame)

    def keep_output(frame, value):
        moved = value.reshape(height, width, channels)
        out_ref[frame] = x_ref[frame] + moved + bias[...].reshape(1, 1, channels)

    feat_load.wait()
    for load in lane_load:
        load.wait()
    local_stats(0, x_ref)
    pack_edges(0, x_ref)
    pl.semaphore_wait(barrier, n_all - 1)
    for_sends(0, x_ref, lambda c: c.start())
    start_stats(0)
    send_front(0, x_ref, 1)
    send_front(0, x_ref, 0)
    layer_pass(0, x_ref, gain1, shift1, lambda: convert(1), keep_hidden)
    local_stats(1, hid_ref)
    start_stats(1)
    pack_edges(1, hid_ref)
    for_sends(1, hid_ref, lambda c: c.start())
    layer_pass(1, hid_ref, gain2, shift2, lambda: None, keep_output)

    for layer, source in enumerate((x_ref, hid_ref)):
        stat_wait(layer).wait_send()
        for_sends(layer, source, lambda c: c.wait_send())

        @pl.when(tm + 1 < n_tm)
        def _():
            for frame in range(frames):
                front_copy(layer, source, frame).wait_send()


def local(counts, features, gain1, shift1, weight1, gain2, shift2, weight2, bias):
    n_tm, n_row, n_col = counts
    frames, height, width, channels = features.shape
    taps = 9 * channels
    lane = lambda v: v.reshape(1, channels)
    weights = lambda w: w.reshape(3, taps, channels)
    vmem = pl.BlockSpec(memory_space=pltpu.VMEM)
    hbm = pl.BlockSpec(memory_space=pltpu.HBM)
    padded = (2 * frames, height + 2, width, 3 * channels)
    dma = pltpu.SemaphoreType.DMA
    return pl.pallas_call(
        functools.partial(kernel, counts),
        out_shape=jax.ShapeDtypeStruct(features.shape, F32),
        in_specs=[hbm] * 8,
        out_specs=vmem,
        scratch_shapes=[
            pltpu.VMEM((5, 1, channels), F32),
            pltpu.VMEM(features.shape, F32),
            pltpu.VMEM(features.shape, F32),
            pltpu.VMEM((2, 3, taps, channels), F32),
            pltpu.VMEM((2, 3, taps, 2 * channels), BF16),
            pltpu.VMEM(padded, BF16),
            pltpu.VMEM(padded, BF16),
            pltpu.VMEM((2, height * width, channels), F32),
            pltpu.VMEM((2, 2, frames, height, channels), F32),
            pltpu.VMEM((2, 2, 2, 8, channels), F32),
            pltpu.VMEM((2, *features.shape), F32),
            pltpu.VMEM((2, 2, 2, frames, width, channels), F32),
            pltpu.VMEM((2, 2, 2, frames, height, channels), F32),
            pltpu.VMEM((2, 2, 2, 2, 8, channels), F32),
            pltpu.VMEM((2, n_tm * n_row * n_col, 2, channels), F32),
            dma((8,)),
            dma((2, len(STEPS))),
            dma((2, len(STEPS))),
            dma((2, frames)),
            dma((2, frames)),
            dma((2,)),
            dma((2,)),
        ],
        compiler_params=pltpu.CompilerParams(
            collective_id=0, has_side_effects=True, vmem_limit_bytes=60 * 1024 * 1024
        ),
    )(features, lane(gain1), lane(shift1), weights(weight1), lane(gain2), lane(shift2), weights(weight2), lane(bias))


def solution(mesh):
    counts = tuple(mesh.shape[axis] for axis in ("tm", "row", "col"))
    in_specs = (P("tm", "row", "col", None), P(), P(), P(), P(), P(), P(), P())
    out_specs = P("tm", "row", "col", None)
    return jax.shard_map(
        functools.partial(local, counts), mesh=mesh, in_specs=in_specs, out_specs=out_specs, check_vma=False
    )
```

time: 37.8 us -> 29.9 us (0.79)
  local copies, waits for them, and re-layouts: 7.88 us -> 1.67 us
  Pallas kernels: 29.7 us -> 28 us
    unnamed x17 -> x1, local copies, waits for them, and re-layouts: 7.88 us -> 1.67 us
    pallas_call x1, Pallas kernels: 29.7 us -> 28 us  [local(): pl.pallas_call(functools.partial(kernel, counts), out_shape=jax.ShapeDtyp...]
where the time goes in v2:
time: 29.9 us; the launch traced here: 29.7 us
  Pallas kernels  28 us (94%)
  local copies, waits for them, and re-layouts  1.67 us (6%)
    pallas_call x1, Pallas kernels, local(): pl.pallas_call(functools.partial(kernel, counts), out_shape=jax.ShapeDtyp...  28 us
    unnamed x1, local copies, waits for them, and re-layouts  1.67 us

profile of v2, /device:TPU:0, one launch (start us, length us, event | category | flops | bytes accessed | tf_op | source)
XLA Modules:
  0.0 29.7 jit_solution(16204016727402773082)
XLA Ops:
  0.0 28.0 %shard_map.82 = f32[2,8,32,128]{3,2,1,0:T(8,128)} custom-call(f32[2,8,32,128]{3,2,1,0:T(8,128)} %feat_hbm.1, f32[1,128]{1,0:T(1,128)} %bitcast.9, f32[1,128]{1,0:T(1,128)} %bitcast.10, f32[3,1152,128]{2,1,0:T(8,128)} %bitcast.7, f32[1,128]{1,0:T(1,128)} %bitcast.11, f32[1,128]{1,0:T(1,128)} %bitcast.12, f32[3,1152,128]{2,1,0:T(8,128)} %bitcast.8, ...), custom_call_target="tpu_custom_call" | custom-call | tf_op jit(solution)/shard_map/pallas_call | solution.py:350
  28.0 1.7 %copy.10 = f32[2,8,32,128]{3,2,1,0:T(8,128)} copy(f32[2,8,32,128]{3,2,1,0:T(8,128)} %shard_map.82) | data formatting | bytes 524288

commit v3 on v2

--- a/solution.py
+++ b/solution.py
@@ -132,7 +132,6 @@
     def for_sends(layer, source, act):
         for k, step in enumerate(STEPS):
 
-
             @pl.when(exists(*step))
             def _():
                 act(halo_copy(layer, source, k))
@@ -256,6 +255,16 @@
         out_second = fold(dot(h, w[second][...])) + both[:, channels:]
         return fold(dot(h, w[first][...])) + both[:, :channels], out_second
 
+    def conv_own(layer):
+        w = [w_split.at[layer, dt] for dt in range(3)]
+        size = height * width
+        first = lines(high, 2)
+        shared = fold(dot(jnp.concatenate([first, lines(high, 3)], axis=0), w[2][...]))
+        lows = jnp.concatenate([lines(low, 2), lines(low, 3)], axis=0)
+        both = dot(lows, jnp.concatenate([w[2][:, :channels], w[1][:, :channels]], axis=1))
+        out_second = shared[size:] + fold(dot(first, w[1][...])) + both[:size, channels:] + both[size:, :channels]
+        return shared[:size] + both[:size, :channels], out_second
+
     def conv_one(layer, frame, dt):
         w = w_split.at[layer, dt]
         return fold(dot(lines(high, frame), w[...])) + dot(lines(low, frame), w[:, :channels])
@@ -279,8 +288,7 @@
         wait_halo(layer, source, 0)
         for frame in range(frames):
             spread_frame(layer, source, 0, frame, activate)
-        part[0], part[1] = conv_pair(layer, 2, True)
-        part[1] += conv_one(layer, 3, 2)
+        part[0], part[1] = conv_own(layer)
         beside()
         wait_halo(layer, source, 1)
 
@@ -304,7 +312,8 @@
 
     def keep_hidden(frame, value):
         hid_ref[frame] = value.reshape(height, width, channels)
-        send_front(1, hid_ref, frame)
+        if frame == 1:
+            send_front(1, hid_ref, 1)
 
     def keep_output(frame, value):
         moved = value.reshape(height, width, channels)
@@ -316,15 +325,16 @@
     local_stats(0, x_ref)
     pack_edges(0, x_ref)
     pl.semaphore_wait(barrier, n_all - 1)
-    for_sends(0, x_ref, lambda c: c.start())
     start_stats(0)
     send_front(0, x_ref, 1)
+    for_sends(0, x_ref, lambda c: c.start())
     send_front(0, x_ref, 0)
     layer_pass(0, x_ref, gain1, shift1, lambda: convert(1), keep_hidden)
     local_stats(1, hid_ref)
     start_stats(1)
     pack_edges(1, hid_ref)
     for_sends(1, hid_ref, lambda c: c.start())
+    send_front(1, hid_ref, 0)
     layer_pass(1, hid_ref, gain2, shift2, lambda: None, keep_output)
 
     for layer, source in enumerate((x_ref, hid_ref)):

time: 29.9 us -> 27.8 us (0.930)
  Pallas kernels: 28 us -> 25.9 us
    pallas_call x1, Pallas kernels: 28 us -> 25.9 us  [local(): pl.pallas_call(functools.partial(kernel, counts), out_shape=jax.ShapeDtyp...]
where the time goes in v3:
time: 27.8 us; the launch traced here: 27.6 us
  Pallas kernels  25.9 us (93%)
  local copies, waits for them, and re-layouts  1.67 us (6%)
    pallas_call x1, Pallas kernels, local(): pl.pallas_call(functools.partial(kernel, counts), out_shape=jax.ShapeDtyp...  25.9 us
    unnamed x1, local copies, waits for them, and re-layouts  1.67 us

profile of v3, /device:TPU:0, one launch (start us, length us, event | category | flops | bytes accessed | tf_op | source)
XLA Modules:
  0.0 27.6 jit_solution(7205733646987526872)
XLA Ops:
  0.0 25.9 %shard_map.82 = f32[2,8,32,128]{3,2,1,0:T(8,128)} custom-call(f32[2,8,32,128]{3,2,1,0:T(8,128)} %feat_hbm.1, f32[1,128]{1,0:T(1,128)} %bitcast.9, f32[1,128]{1,0:T(1,128)} %bitcast.10, f32[3,1152,128]{2,1,0:T(8,128)} %bitcast.7, f32[1,128]{1,0:T(1,128)} %bitcast.11, f32[1,128]{1,0:T(1,128)} %bitcast.12, f32[3,1152,128]{2,1,0:T(8,128)} %bitcast.8, ...), custom_call_target="tpu_custom_call" | custom-call | tf_op jit(solution)/shard_map/pallas_call | solution.py:360
  25.9 1.7 %copy.10 = f32[2,8,32,128]{3,2,1,0:T(8,128)} copy(f32[2,8,32,128]{3,2,1,0:T(8,128)} %shard_map.82) | data formatting | bytes 524288

commit v4 on v3

--- a/solution.py
+++ b/solution.py
@@ -1,4 +1,5 @@
 import functools
+import itertools
 import jax
 import jax.numpy as jnp
 from jax import lax
@@ -18,14 +19,6 @@
     for right in (-1, 0, 1)
     if (down, right) != (0, 0)
 ]
-
-
-def repeat(count, body):
-    if count <= 4:
-        for i in range(count):
-            body(i)
-    else:
-        lax.fori_loop(0, count, lambda i, _: (body(i), 0)[1], 0)
 
 
 def group_total(value):
@@ -84,12 +77,21 @@
 
     barrier = pltpu.get_barrier_semaphore()
 
-    def greet(i):
-        pl.semaphore_signal(
-            barrier, inc=1, device_id=place(lax.rem(rank + 1 + i, n_all)), device_id_type=MESH
-        )
-
-    repeat(n_all - 1, greet)
+    def ring(at, step, count):
+        return jnp.where(at + step >= count, at + step - count, at + step)
+
+    def for_others(body):
+        if n_all <= 32:
+            for steps in itertools.product(range(n_tm), range(n_row), range(n_col)):
+                if any(steps):
+                    body(tuple(ring(*each) for each in zip((tm, row, col), steps, counts)))
+        else:
+            lax.fori_loop(1, n_all, lambda i, _: (body(place(lax.rem(rank + i, n_all))), 0)[1], 0)
+
+    def greet(other):
+        pl.semaphore_signal(barrier, inc=1, device_id=other, device_id_type=MESH)
+
+    for_others(greet)
 
     def halo_copy(layer, source, k):
         ahead, down, right = STEPS[k]
@@ -156,14 +158,13 @@
                     if h in (0, height - 1):
                         corners[layer, 0 if h else 1, c_side, frame : frame + 1, :] = line
 
-    def stat_copy(layer, i):
-        to = lax.rem(rank + 1 + i, n_all)
+    def stat_copy(layer, other):
         return pltpu.make_async_remote_copy(
             src_ref=stats.at[layer, rank],
             dst_ref=stats.at[layer, rank],
             send_sem=stat_send.at[layer],
             recv_sem=stat_recv.at[layer],
-            device_id=place(to),
+            device_id=other,
             device_id_type=MESH,
         )
 
@@ -270,7 +271,7 @@
         return fold(dot(lines(high, frame), w[...])) + dot(lines(low, frame), w[:, :channels])
 
     def start_stats(layer):
-        repeat(n_all - 1, lambda i: stat_copy(layer, i).start())
+        for_others(lambda other: stat_copy(layer, other).start())
 
     def layer_pass(layer, source, gain, shift, beside, emit):
         if layer == 0:

time: 27.8 us -> 27.2 us (0.978)
  Pallas kernels: 25.9 us -> 25.4 us
    pallas_call x1, Pallas kernels: 25.9 us -> 25.4 us  [local(): pl.pallas_call(functools.partial(kernel, counts), out_shape=jax.ShapeDtyp...]
where the time goes in v4:
time: 27.2 us; the launch traced here: 27.1 us
  Pallas kernels  25.4 us (93%)
  local copies, waits for them, and re-layouts  1.67 us (6%)
    pallas_call x1, Pallas kernels, local(): pl.pallas_call(functools.partial(kernel, counts), out_shape=jax.ShapeDtyp...  25.4 us
    unnamed x1, local copies, waits for them, and re-layouts  1.67 us

profile of v4, /device:TPU:0, one launch (start us, length us, event | category | flops | bytes accessed | tf_op | source)
XLA Modules:
  0.0 27.1 jit_solution(6606079962077917417)
XLA Ops:
  0.0 25.4 %shard_map.82 = f32[2,8,32,128]{3,2,1,0:T(8,128)} custom-call(f32[2,8,32,128]{3,2,1,0:T(8,128)} %feat_hbm.1, f32[1,128]{1,0:T(1,128)} %bitcast.9, f32[1,128]{1,0:T(1,128)} %bitcast.10, f32[3,1152,128]{2,1,0:T(8,128)} %bitcast.7, f32[1,128]{1,0:T(1,128)} %bitcast.11, f32[1,128]{1,0:T(1,128)} %bitcast.12, f32[3,1152,128]{2,1,0:T(8,128)} %bitcast.8, ...), custom_call_target="tpu_custom_call" | custom-call | tf_op jit(solution)/shard_map/pallas_call | solution.py:361
  25.4 1.7 %copy.10 = f32[2,8,32,128]{3,2,1,0:T(8,128)} copy(f32[2,8,32,128]{3,2,1,0:T(8,128)} %shard_map.82) | data formatting | bytes 524288
